TPU v7x, 128 devices: a whole 4x4x4 slice. The times are simulated.
128 devices in a mesh: dp: 8 (over z, core), seq: 16 (over x, y).
Axes of the slice: x: 4, y: 4, z: 4, core: 2. Of those that a mesh axis runs over, the one named last changes fastest.
Arguments:
- q_raw: bfloat16 [8, 4096, 2048], P('dp', 'seq'), may hold values from -12 to 12
- k_raw: bfloat16 [8, 4096, 2048], P('dp', 'seq'), may hold values from -12 to 12
- values: bfloat16 [8, 4096, 2048], P('dp', 'seq'), may hold values from -6 to 6
- grad_out: bfloat16 [8, 4096, 2048], P('dp', 'seq'), may hold values from -6 to 6
- segment_ids: int32 [8, 4096], P('dp', 'seq'), may hold values from 0 to 3, never falling along the last dimension, each value on 1 to 2048 neighbouring positions
- row_plan: int32 [8, 4096], P('dp', 'seq'), may hold values from 0 to 4095, each once within a row
- q_gain: float32 [128], replicated, may hold values from 0.5 to 5.5
- k_gain: float32 [128], replicated, may hold values from 0.5 to 5.5
Outputs:
- dq_raw: bfloat16 [8, 4096, 2048], P('dp', 'seq')
- dk_raw: bfloat16 [8, 4096, 2048], P('dp', 'seq')
- dv_orig: bfloat16 [8, 4096, 2048], P('dp', 'seq')
- q_gain_grad: float32 [128], replicated
- k_gain_grad: float32 [128], replicated
Inputs may be any that keep to these rules, and one draw needn't show every extreme that they name: `segment_ids`: clip numbers never fall along a group; each clip spans 1 to 2048 positions, one exactly 2048. `row_plan`: each group's row holds every position once.
All inputs are finite; a program needn't handle non-finite values.
Results may differ from a plain program's by a relative error of at most 0.0044.
The roundings to bfloat16 on the way count: a program that leaves them out, or rounds other values in their place, can miss the bound.
Values may be sent and summed in bfloat16 or wider, within the bound.
A program may use at most 192 MiB of HBM per device.

v0:
```python
import jax
import jax.numpy as jnp
from jax import lax
from jax.sharding import PartitionSpec as P

HD = 128


def shortened(shard):

    def short(part):
        return part.astype(jnp.bfloat16) if part.dtype == jnp.float32 else part

    return jax.tree.map(short, shard)


def normalize(raw, gain):
    full = raw.astype(jnp.float32)
    rms = lax.rsqrt(jnp.mean(full * full, axis=-1, keepdims=True) + 1e-06)
    normed_hat = full * rms
    return (normed_hat, rms, (normed_hat * gain).astype(jnp.bfloat16))


def denormalize(d_norm, normed_hat, rms, gain):
    d_hat = d_norm * gain
    gain_part = jnp.sum(d_norm * normed_hat, axis=(0, 1))
    d_raw = rms * (d_hat - normed_hat * jnp.mean(d_hat * normed_hat, axis=-1, keepdims=True))
    return (d_raw.astype(jnp.bfloat16), gain_part)


def head_grad(q_norm, k_norm, value_rows, dout_rows, clip_ids):
    seq_length = q_norm.shape[0]
    width = q_norm.shape[1]
    factor = width ** (-0.5)
    block = min(1024, seq_length)
    count = seq_length // block
    blocked = lambda a: a.reshape((count, block) + a.shape[1:])

    def step(carry, items):
        dk_total, dv_total = carry
        q_block, d_block, c_block = items
        scores = jnp.dot(q_block, k_norm.T, preferred_element_type=jnp.float32) * factor
        same_clip = c_block[:, None] == clip_ids[None, :]
        scores = jnp.where(same_clip, scores, -jnp.inf)
        top_score = jnp.max(scores, axis=1, keepdims=True)
        weights = jnp.exp(scores - top_score)
        probs = weights / jnp.sum(weights, axis=1, keepdims=True)
        probs_b = probs.astype(jnp.bfloat16)
        dv_total = dv_total + jnp.dot(probs_b.T, d_block, preferred_element_type=jnp.float32)
        d_probs = jnp.dot(d_block, value_rows.T, preferred_element_type=jnp.float32)
        delta = jnp.sum(d_probs * probs, axis=1, keepdims=True)
        d_scores = (probs * (d_probs - delta) * factor).astype(jnp.bfloat16)
        dq_block = jnp.dot(d_scores, k_norm, preferred_element_type=jnp.float32)
        dk_total = dk_total + jnp.dot(d_scores.T, q_block, preferred_element_type=jnp.float32)
        return ((dk_total, dv_total), dq_block)

    empty = jnp.zeros((seq_length, width), jnp.float32)
    (dk_norm, dv_total), dq_blocks = lax.scan(
        step, (empty, empty), (blocked(q_norm), blocked(dout_rows), blocked(clip_ids))
    )
    return (dq_blocks.reshape(seq_length, width), dk_norm, dv_total.astype(jnp.bfloat16))


def on_device(q_raw, k_raw, values, grad_out, segment_ids, row_plan, q_gain, k_gain):
    head_q, head_k, head_v, head_d = (
        lax.all_to_all(q_raw, "seq", split_axis=2, concat_axis=1, tiled=True),
        lax.all_to_all(k_raw, "seq", split_axis=2, concat_axis=1, tiled=True),
        lax.all_to_all(values, "seq", split_axis=2, concat_axis=1, tiled=True),
        lax.all_to_all(grad_out, "seq", split_axis=2, concat_axis=1, tiled=True),
    )
    clip_all, plan_all = (
        lax.all_gather(segment_ids, "seq", axis=1, tiled=True),
        lax.all_gather(row_plan, "seq", axis=1, tiled=True),
    )
    clip_ids = clip_all[0]
    seq_length = head_q.shape[1]
    local_heads = head_q.shape[2] // HD
    inverse = (
        jnp.zeros((seq_length,), jnp.int32)
        .at[plan_all[0]]
        .set(jnp.arange(seq_length, dtype=jnp.int32))
    )
    shaped = lambda a: a[0].reshape(seq_length, local_heads, HD)
    heads_first = lambda a: a.transpose(1, 0, 2)
    q_hat, q_rms, q_norm = normalize(shaped(head_q), q_gain)
    k_hat, k_rms, k_norm = normalize(shaped(head_k), k_gain)
    dq_norm, dk_norm, d_value = lax.map(
        lambda part: head_grad(part[0], part[1], part[2], part[3], clip_ids),
        (
            heads_first(q_norm),
            heads_first(k_norm),
            heads_first(shaped(head_v)),
            heads_first(shaped(head_d)),
        ),
    )
    d_query, gain_q_part = denormalize(heads_first(dq_norm), q_hat, q_rms, q_gain)
    d_key, gain_k_part = denormalize(heads_first(dk_norm), k_hat, k_rms, k_gain)
    gain_q, gain_k = lax.psum((gain_q_part, gain_k_part), ("dp", "seq"))
    flatten = lambda a: a.reshape(1, seq_length, local_heads * HD)
    pieces = (flatten(d_query), flatten(d_key), flatten(heads_first(d_value)))
    pieces = tuple((item[:, inverse] for item in pieces))
    back_q, back_k, back_v = jax.tree.map(
        lambda part, own: part.astype(own.dtype),
        lax.all_to_all(shortened(pieces), "seq", split_axis=1, concat_axis=2, tiled=True),
        pieces,
    )
    return (back_q, back_k, back_v, gain_q, gain_k)


def solution(mesh):
    placed = (
        P("dp", "seq", None),
        P("dp", "seq", None),
        P("dp", "seq", None),
        P("dp", "seq", None),
        P("dp", "seq"),
        P("dp", "seq"),
        P(),
        P(),
    )
    return jax.shard_map(
        on_device,
        mesh=mesh,
        in_specs=placed,
        out_specs=(P("dp", "seq", None), P("dp", "seq", None), P("dp", "seq", None), P(), P()),
        check_vma=False,
    )
```

profile of v0, /device:TPU:1, one launch (start us, length us, event | category | flops | bytes accessed | tf_op | source)
XLA Modules:
  0.0 758.8 jit_solution(15193959619286929670)
XLA Ops:
  5.8 10.6 %reduce.16 = bf16[2048,256]{1,0:T(8,128)(2,1)S(1)} reduce(bf16[2048,1,256]{2,1,0:T(2,128)(2,1)S(1)} %bitcast.161, bf16[]{:T(256)} %broadcast.255), dimensions={1}, to_apply=%bitcast.90.reduce_sub_computation | reduce | bytes 2097154
  17.5 7.6 all-to-all-start
  25.1 5.9 copy.88
  31.0 12.6 %reduce.17 = bf16[2048,256]{1,0:T(8,128)(2,1)} reduce(bf16[2048,1,256]{2,1,0:T(2,128)(2,1)} %bitcast.166, bf16[]{:T(256)} %broadcast.255), dimensions={1}, to_apply=%bitcast.92.reduce_sub_computation | reduce | bytes 2097154
  45.8 5.9 copy.93
  51.7 12.6 %reduce.18 = bf16[2048,256]{1,0:T(8,128)(2,1)} reduce(bf16[2048,1,256]{2,1,0:T(2,128)(2,1)} %bitcast.167, bf16[]{:T(256)} %broadcast.255), dimensions={1}, to_apply=%bitcast.94.reduce_sub_computation | reduce | bytes 2097154
  66.4 5.9 copy.95
  72.4 12.6 %reduce.19 = bf16[2048,256]{1,0:T(8,128)(2,1)} reduce(bf16[2048,1,256]{2,1,0:T(2,128)(2,1)} %bitcast.168, bf16[]{:T(256)} %broadcast.255), dimensions={1}, to_apply=%bitcast.96.reduce_sub_computation | reduce | bytes 2097154
  87.2 17.9 %all_gather.6 = s32[1,4096]{1,0:T(1,128)S(1)} all-gather(s32[1,256]{1,0:T(1,128)S(1)} %copy-done.17), channel_id=1, replica_groups=mesh['dp'=8,'seq'=16] {'seq'}, dimensions={1}, use_global_device_ids=true | all-gather | bytes 17408 | tf_op jit(solution)/shard_map/all_gather | solution.py:72
  106.3 17.4 %all_gather.7 = s32[1,4096]{1,0:T(1,128)S(1)} all-gather(s32[1,256]{1,0:T(1,128)S(1)} %copy-done.18), channel_id=1, replica_groups=mesh['dp'=8,'seq'=16] {'seq'}, dimensions={1}, use_global_device_ids=true | all-gather | bytes 17408 | tf_op jit(solution)/shard_map/all_gather | solution.py:73
  128.1 15.5 %scatter_custom_fusion = s32[4096]{0:T(1024)S(1)} fusion(s32[4096]{0:T(1024)S(1)} %bitcast.193, s32[4096]{0:T(1024)S(1)} %iota.3, s32[]{:T(128)} %constant.51.clone.1), kind=kCustom, calls=%fused_computation.58 | custom fusion | bytes 16388 | tf_op jit(solution)/shard_map/scatter | solution.py:81
  147.7 6.5 all-to-all-start.2
  154.3 5.8 reshape.417
  166.0 5.4 all-to-all-start.3
  195.3 5.8 reshape.421
  210.7 259.3 %while.26 = (s32[]{:T(128)}, f32[4096,128]{1,0:T(8,128)S(1)}, f32[4096,128]{1,0:T(8,128)}, f32[4,1024,128]{2,1,0:T(8,128)}, s32[4,1024]{1,0:T(4,128)S(1)}, /*ind...) while((s32[]{:T(128)}, f32[4096,128]{1,0:T(8,128)S(1)}, ...), condition=%wide.region_6.7_spmd.clone, body=%wide.region_2.6_spmd.clone.sunk | while | flops 5458883584 | bytes 306808512 | solution.py:58
  214.9 4.7 fusion.61
  220.5 18.3 %multiply_reduce_fusion.6 = (f32[1024]{0:T(1024)S(1)}, f32[1024,4096]{1,0:T(8,128)}, f32[1024,4096]{1,0:T(8,128)}) fusion(f32[1024]{0:T(1024)S(1)} %fusion.61, f32[1024]{0:T(1024)S(1)} %get-tuple-element.232, f32[1024,4096]{1,0:T(8,128)} %copy-done.1, s32[4096]{0:T(1024)S(1)} %bitcast.184, s32[1024]{0:T(1024)S(1)} %bitcast.187, ...), kind=kOutput, calls=%fused_computation.5.clone.1 | convolution fusion | flops 1103100928 | bytes 51675140 | tf_op jit(solution)/shard_map/while/body/eval_jaxpr/while/body/eval_jaxpr/dot_general | solution.py:50
  238.8 15.2 %multiply_convert_fusion.5 = bf16[1024,4096]{1,0:T(8,128)(2,1)} fusion(f32[1024,4096]{1,0:T(8,128)} %get-tuple-element.233, f32[1024,4096]{1,0:T(8,128)} %get-tuple-element.234, f32[1024]{0:T(1024)S(1)} %get-tuple-element.235), kind=kLoop, calls=%fused_computation.4.clone.1 | loop fusion | flops 16777216 | bytes 41947136 | tf_op jit(solution)/shard_map/while/body/eval_jaxpr/while/body/eval_jaxpr/convert_element_type | solution.py:52
  254.1 6.4 convolution_add_fusion.2
  260.5 7.5 fusion.63
  281.6 18.3 %multiply_reduce_fusion.6 = (f32[1024]{0:T(1024)S(1)}, f32[1024,4096]{1,0:T(8,128)}, f32[1024,4096]{1,0:T(8,128)}) fusion(f32[1024]{0:T(1024)S(1)} %fusion.61, f32[1024]{0:T(1024)S(1)} %get-tuple-element.232, f32[1024,4096]{1,0:T(8,128)} %copy-done.1, s32[4096]{0:T(1024)S(1)} %bitcast.184, s32[1024]{0:T(1024)S(1)} %bitcast.187, ...), kind=kOutput, calls=%fused_computation.5.clone.1 | convolution fusion | flops 1103100928 | bytes 51675140 | tf_op jit(solution)/shard_map/while/body/eval_jaxpr/while/body/eval_jaxpr/dot_general | solution.py:50
  299.9 15.2 %multiply_convert_fusion.5 = bf16[1024,4096]{1,0:T(8,128)(2,1)} fusion(f32[1024,4096]{1,0:T(8,128)} %get-tuple-element.233, f32[1024,4096]{1,0:T(8,128)} %get-tuple-element.234, f32[1024]{0:T(1024)S(1)} %get-tuple-element.235), kind=kLoop, calls=%fused_computation.4.clone.1 | loop fusion | flops 16777216 | bytes 41947136 | tf_op jit(solution)/shard_map/while/body/eval_jaxpr/while/body/eval_jaxpr/convert_element_type | solution.py:52
  315.1 6.4 convolution_add_fusion.2
  321.6 7.5 fusion.63
  329.1 5.3 fusion.62
  344.3 18.3 %multiply_reduce_fusion.6 = (f32[1024]{0:T(1024)S(1)}, f32[1024,4096]{1,0:T(8,128)}, f32[1024,4096]{1,0:T(8,128)}) fusion(f32[1024]{0:T(1024)S(1)} %fusion.61, f32[1024]{0:T(1024)S(1)} %get-tuple-element.232, f32[1024,4096]{1,0:T(8,128)} %copy-done.1, s32[4096]{0:T(1024)S(1)} %bitcast.184, s32[1024]{0:T(1024)S(1)} %bitcast.187, ...), kind=kOutput, calls=%fused_computation.5.clone.1 | convolution fusion | flops 1103100928 | bytes 51675140 | tf_op jit(solution)/shard_map/while/body/eval_jaxpr/while/body/eval_jaxpr/dot_general | solution.py:50
  362.6 15.2 %multiply_convert_fusion.5 = bf16[1024,4096]{1,0:T(8,128)(2,1)} fusion(f32[1024,4096]{1,0:T(8,128)} %get-tuple-element.233, f32[1024,4096]{1,0:T(8,128)} %get-tuple-element.234, f32[1024]{0:T(1024)S(1)} %get-tuple-element.235), kind=kLoop, calls=%fused_computation.4.clone.1 | loop fusion | flops 16777216 | bytes 41947136 | tf_op jit(solution)/shard_map/while/body/eval_jaxpr/while/body/eval_jaxpr/convert_element_type | solution.py:52
  377.8 6.4 convolution_add_fusion.2
  384.2 7.5 fusion.63
  391.7 5.3 fusion.62
  406.9 18.3 %multiply_reduce_fusion.6 = (f32[1024]{0:T(1024)S(1)}, f32[1024,4096]{1,0:T(8,128)}, f32[1024,4096]{1,0:T(8,128)}) fusion(f32[1024]{0:T(1024)S(1)} %fusion.61, f32[1024]{0:T(1024)S(1)} %get-tuple-element.232, f32[1024,4096]{1,0:T(8,128)} %copy-done.1, s32[4096]{0:T(1024)S(1)} %bitcast.184, s32[1024]{0:T(1024)S(1)} %bitcast.187, ...), kind=kOutput, calls=%fused_computation.5.clone.1 | convolution fusion | flops 1103100928 | bytes 51675140 | tf_op jit(solution)/shard_map/while/body/eval_jaxpr/while/body/eval_jaxpr/dot_general | solution.py:50
  425.2 15.2 %multiply_convert_fusion.5 = bf16[1024,4096]{1,0:T(8,128)(2,1)} fusion(f32[1024,4096]{1,0:T(8,128)} %get-tuple-element.233, f32[1024,4096]{1,0:T(8,128)} %get-tuple-element.234, f32[1024]{0:T(1024)S(1)} %get-tuple-element.235), kind=kLoop, calls=%fused_computation.4.clone.1 | loop fusion | flops 16777216 | bytes 41947136 | tf_op jit(solution)/shard_map/while/body/eval_jaxpr/while/body/eval_jaxpr/convert_element_type | solution.py:52
  440.4 6.4 convolution_add_fusion.2
  446.9 7.5 fusion.63
  454.3 5.3 fusion.62
  475.0 15.0 %gather_fusion.1 = bf16[4096,128]{1,0:T(8,128)(2,1)} fusion(bf16[4096,128]{1,0:T(8,128)(2,1)S(1)} %multiply_convert_fusion.1, s32[4096]{0:T(1024)S(1)} %copy-done.7), kind=kCustom, calls=%fused_computation.1 | custom fusion | bytes 2113536 | tf_op jit(solution)/shard_map/gather | solution.py:101
  493.2 23.4 %reduce.21 = bf16[4096,128]{1,0:T(8,128)(2,1)} reduce(bf16[4096,1,128]{2,1,0:T(2,128)(2,1)S(1)} %bitcast.164, bf16[]{:T(256)} %broadcast.255), dimensions={1}, to_apply=%bitcast.118.reduce_sub_computation | reduce | bytes 2097154
  518.9 6.7 all-to-all-start.5
  530.7 12.1 %gather_fusion = bf16[4096,128]{1,0:T(8,128)(2,1)S(1)} fusion(bf16[4096,128]{1,0:T(8,128)(2,1)S(1)} %bitcast.145, s32[4096]{0:T(1024)S(1)} %copy-done.7), kind=kCustom, calls=%fused_computation | custom fusion | bytes 2113536 | tf_op jit(solution)/shard_map/gather | solution.py:101
  542.8 16.7 %copy.129 = bf16[1,4096,128]{2,0,1:T(2,128)(2,1)S(1)} copy(bf16[1,4096,128]{2,1,0:T(8,128)(2,1)S(1)} %bitcast.172) | data formatting | bytes 2097152 | tf_op jit(solution)/shard_map/gather | solution.py:101
  559.6 22.4 %reduce.20 = bf16[4096,128]{1,0:T(8,128)(2,1)S(1)} reduce(bf16[4096,1,128]{2,1,0:T(2,128)(2,1)S(1)} %bitcast.165, bf16[]{:T(256)} %broadcast.255), dimensions={1}, to_apply=%bitcast.119.reduce_sub_computation | reduce | bytes 2097154
  583.1 6.9 all-to-all-start.4
  591.6 12.1 %gather_fusion.2 = bf16[4096,128]{1,0:T(8,128)(2,1)S(1)} fusion(bf16[4096,128]{1,0:T(8,128)(2,1)S(1)} %convert_element_type.115, s32[4096]{0:T(1024)S(1)} %copy-done.7), kind=kCustom, calls=%fused_computation.2 | custom fusion | bytes 2113536 | tf_op jit(solution)/shard_map/gather | solution.py:101
  603.8 16.7 %copy.127 = bf16[1,4096,128]{2,0,1:T(2,128)(2,1)S(1)} copy(bf16[1,4096,128]{2,1,0:T(8,128)(2,1)S(1)} %bitcast.170) | data formatting | bytes 2097152 | tf_op jit(solution)/shard_map/gather | solution.py:101
  620.5 22.4 %reduce.22 = bf16[4096,128]{1,0:T(8,128)(2,1)S(1)} reduce(bf16[4096,1,128]{2,1,0:T(2,128)(2,1)S(1)} %bitcast.163, bf16[]{:T(256)} %broadcast.255), dimensions={1}, to_apply=%bitcast.117.reduce_sub_computation | reduce | bytes 2097154
  644.1 6.8 all-to-all-start.6
  650.8 87.7 %all-reduce = (f32[128]{0:T(128)}, f32[128]{0:T(128)}) all-reduce(f32[128]{0:T(128)S(1)} %get-tuple-element.134, f32[128]{0:T(128)S(1)} %get-tuple-element.132), channel_id=1, replica_groups=mesh['dp'=8,'seq'=16] {'dp','seq'}, use_global_device_ids=true, to_apply=%region_11.12 | all-reduce | flops 256 | bytes 2048 | tf_op jit(solution)/shard_map/psum | solution.py:98
  (130 shorter events, 139.5 us)
Async XLA Ops:
  17.5 106.3 %all-to-all-start = ((bf16[16,2,16384]{2,1,0:T(2,128)(2,1)}), bf16[16,2,16384]{2,1,0:T(2,128)(2,1)S(1)}, u32[]{:S(2)}, u32[]{:S(2)}) async-start(bf16[16,2,16384]{2,1,0:T(2,128)(2,1)} %reshape.414), calls=%async_computation | async-start | bytes 2097152 | tf_op jit(solution)/shard_map/all_to_all | solution.py:66
  72.4 14.9 %copy-start.17 = (s32[1,256]{1,0:T(1,128)S(1)}, s32[1,256]{1,0:T(1,128)}, u32[]{:S(2)}) copy-start(s32[1,256]{1,0:T(1,128)} %param.14) | copy-start | bytes 3076
  72.4 34.0 %copy-start.18 = (s32[1,256]{1,0:T(1,128)S(1)}, s32[1,256]{1,0:T(1,128)}, u32[]{:S(2)}) copy-start(s32[1,256]{1,0:T(1,128)} %param.15) | copy-start | bytes 3076
  123.7 24.0 %all-to-all-start.1 = ((bf16[16,2,16384]{2,1,0:T(2,128)(2,1)}), bf16[16,2,16384]{2,1,0:T(2,128)(2,1)}, u32[]{:S(2)}, u32[]{:S(2)}) async-start(bf16[16,2,16384]{2,1,0:T(2,128)(2,1)} %reshape.416), calls=%async_computation.1 | async-start | bytes 2097152 | tf_op jit(solution)/shard_map/all_to_all | solution.py:67
  147.7 18.3 %all-to-all-start.2 = ((bf16[16,2,16384]{2,1,0:T(2,128)(2,1)}), bf16[16,2,16384]{2,1,0:T(2,128)(2,1)S(1)}, u32[]{:S(2)}, u32[]{:S(2)}) async-start(bf16[16,2,16384]{2,1,0:T(2,128)(2,1)} %reshape.418), calls=%async_computation.2 | async-start | bytes 2097152 | tf_op jit(solution)/shard_map/all_to_all | solution.py:69
  160.0 3.2 copy-start.5
  166.0 29.3 %all-to-all-start.3 = ((bf16[16,2,16384]{2,1,0:T(2,128)(2,1)}), bf16[16,2,16384]{2,1,0:T(2,128)(2,1)}, u32[]{:S(2)}, u32[]{:S(2)}) async-start(bf16[16,2,16384]{2,1,0:T(2,128)(2,1)} %reshape.420), calls=%async_computation.3 | async-start | bytes 2097152 | tf_op jit(solution)/shard_map/all_to_all | solution.py:68
  179.7 26.4 %copy-start.10 = (f32[4,1024]{1,0:T(4,128)}, f32[4,1024]{1,0:T(4,128)S(1)}, u32[]{:S(2)}) copy-start(f32[4,1024]{1,0:T(4,128)S(1)} %rsqrt.28) | copy-start | bytes 49156
  187.4 21.6 %copy-start.8 = (f32[2,2,8,128]{3,1,2,0:T(2,128)}, f32[2,2,8,128]{3,1,2,0:T(2,128)S(1)}, u32[]{:S(2)}) copy-start(f32[2,2,8,128]{3,1,2,0:T(2,128)S(1)} %copy.114) | copy-start | bytes 49156
  201.1 5.0 copy-start.15
  206.1 2.9 copy-start.2
  206.1 2.9 copy-start.13
  210.7 259.3 %copy-start.9 = (f32[2,2,8,128]{3,1,2,0:T(2,128)S(1)}, f32[2,2,8,128]{3,1,2,0:T(2,128)}, u32[]{:S(2)}) copy-start(f32[2,2,8,128]{3,1,2,0:T(2,128)} %copy-done.8) | copy-start | bytes 49156
  210.7 259.3 %copy-start.14 = (f32[128]{0:T(128)S(1)}, f32[128]{0:T(128)}, u32[]{:S(2)}) copy-start(f32[128]{0:T(128)} %param.17) | copy-start | bytes 1540
  214.8 5.7 copy-start.1
  254.1 13.9 %copy-start = (f32[1024,4096]{1,0:T(8,128)S(1)}, f32[1024,4096]{1,0:T(8,128)}, u32[]{:S(2)}) copy-start(f32[1024,4096]{1,0:T(8,128)} %get-tuple-element.233) | copy-start | bytes 50331652 | tf_op jit(solution)/shard_map/while/body/eval_jaxpr/while
  275.9 5.7 copy-start.1
  315.1 13.9 %copy-start = (f32[1024,4096]{1,0:T(8,128)S(1)}, f32[1024,4096]{1,0:T(8,128)}, u32[]{:S(2)}) copy-start(f32[1024,4096]{1,0:T(8,128)} %get-tuple-element.233) | copy-start | bytes 50331652 | tf_op jit(solution)/shard_map/while/body/eval_jaxpr/while
  338.6 5.7 copy-start.1
  377.8 13.9 %copy-start = (f32[1024,4096]{1,0:T(8,128)S(1)}, f32[1024,4096]{1,0:T(8,128)}, u32[]{:S(2)}) copy-start(f32[1024,4096]{1,0:T(8,128)} %get-tuple-element.233) | copy-start | bytes 50331652 | tf_op jit(solution)/shard_map/while/body/eval_jaxpr/while
  401.2 5.7 copy-start.1
  440.4 13.9 %copy-start = (f32[1024,4096]{1,0:T(8,128)S(1)}, f32[1024,4096]{1,0:T(8,128)}, u32[]{:S(2)}) copy-start(f32[1024,4096]{1,0:T(8,128)} %get-tuple-element.233) | copy-start | bytes 50331652 | tf_op jit(solution)/shard_map/while/body/eval_jaxpr/while
  469.9 2.7 copy-start.3
  472.6 2.4 copy-start.7
  516.6 9.0 %copy-start.4 = (f32[1,256,16,128]{3,1,2,0:T(8,128)S(1)}, f32[1,256,16,128]{3,1,2,0:T(8,128)}, u32[]{:S(2)}) copy-start(f32[1,256,16,128]{3,1,2,0:T(8,128)} %copy.87) | copy-start | bytes 6291460
  516.6 9.0 %copy-start.11 = (f32[4,1024]{1,0:T(4,128)S(1)}, f32[4,1024]{1,0:T(4,128)}, u32[]{:S(2)}) copy-start(f32[4,1024]{1,0:T(4,128)} %copy-done.10) | copy-start | bytes 49156
  516.6 9.0 %copy-start.16 = (f32[128]{0:T(128)S(1)}, f32[128]{0:T(128)}, u32[]{:S(2)}) copy-start(f32[128]{0:T(128)} %param.16) | copy-start | bytes 1540
  518.9 64.2 %all-to-all-start.5 = ((bf16[16,2,16384]{2,1,0:T(2,128)(2,1)}), bf16[16,2,16384]{2,1,0:T(2,128)(2,1)}, u32[]{:S(2)}, u32[]{:S(2)}) async-start(bf16[16,2,16384]{2,1,0:T(2,128)(2,1)} %reshape.424), calls=%async_computation.5 | async-start | bytes 2097152 | tf_op jit(solution)/shard_map/all_to_all | solution.py:104
  525.6 2.7 copy-start.12
  525.6 2.7 copy-start.6
  583.1 61.0 %all-to-all-start.4 = ((bf16[16,2,16384]{2,1,0:T(2,128)(2,1)}), bf16[16,2,16384]{2,1,0:T(2,128)(2,1)}, u32[]{:S(2)}, u32[]{:S(2)}) async-start(bf16[16,2,16384]{2,1,0:T(2,128)(2,1)} %reshape.422), calls=%async_computation.4 | async-start | bytes 2097152 | tf_op jit(solution)/shard_map/all_to_all | solution.py:104
  644.1 111.2 %all-to-all-start.6 = ((bf16[16,2,16384]{2,1,0:T(2,128)(2,1)}), bf16[16,2,16384]{2,1,0:T(2,128)(2,1)S(1)}, u32[]{:S(2)}, u32[]{:S(2)}) async-start(bf16[16,2,16384]{2,1,0:T(2,128)(2,1)} %reshape.426), calls=%async_computation.6 | async-start | bytes 2097152 | tf_op jit(solution)/shard_map/all_to_all | solution.py:104
where the time goes:
time: 770 us; the launch traced here: 759 us
  other arithmetic  229 us (30%)
  local copies, waits for them, and re-layouts  185 us (24%)
  matrix products  165 us (21%)
  blocking collectives  123 us (16%)
  starting transfers between devices  44.2 us (6%)
  loops' own time  10.3 us (1%)
    unnamed x12, other arithmetic  117 us
    psum x1, blocking collectives, on_device(): gain_q, gain_k = lax.psum((gain_q_part, gain_k_part), ('dp', 'seq'))  87.7 us
    gather x6, local copies, waits for them, and re-layouts, on_device(): pieces = tuple((item[:, inverse] for item in pieces))  75.9 us
    unnamed x64, local copies, waits for them, and re-layouts  75.4 us
    dot_general x4, matrix products, step(): d_probs = jnp.dot(d_block, value_rows.T, preferred_element_type=jnp.float32)  73.1 us
    convert_element_type x4, other arithmetic, step(): d_scores = (probs * (d_probs - delta) * factor).astype(jnp.bfloat16)  60.9 us
    dot_general x4, matrix products, step(): dq_block = jnp.dot(d_scores, k_norm, preferred_element_type=jnp.float32)  30 us
    dot_general x4, matrix products, step(): jnp.dot(d_scores.T, q_block, preferred_element_type=jnp.float32)  25.7 us
  transfers between devices with their start and end apart: 7, of which 1 were waited for; matrix products, arithmetic and copies ran while one was open for 32% of the time, Pallas kernels for 0%

commit v1 on v0

v1 whole, which is shorter than its diff:
```python
import functools
import jax
import jax.numpy as jnp
from jax import lax
from jax.experimental import pallas as pl
from jax.experimental.pallas import tpu as pltpu
from jax.sharding import PartitionSpec as P

HD = 128
BLK = 256
BIG = -1e30
LOG2E = 1.4426950408889634
MESH = pl.DeviceIdType.MESH
NT = (((1,), (1,)), ((), ()))


def rows_mean(x):
    return jnp.sum(x, axis=1, keepdims=True) * (1.0 / HD)


def fold(x):
    return x.reshape(x.shape[0] // 8, 8, x.shape[1])


def kernel(
    nx, ny, ndp,
    q_in, k_in, d_in, v_in, seg_in, plan_in, qg_in, kg_in,
    oq, ok, ov, gq_out, gk_out,
    rq, rk, rd, rv, meta_src, meta, fbuf,
    raw_q, raw_k, qaug, kaug, k_t, dor, vr,
    wbuf, inv_ref, dp_ref, dvf, dkf, pair, stage, stage2,
    idx_v, idx_s, gpart, gsum, gbuf1, gbuf2,
    in_send, in_recv, meta_send, meta_recv, out_send, out_recv,
    g1_send, g1_recv, g2_send, g2_recv, loc_sem, oloc_sem, idx_sem,
):
    n = nx * ny
    length = n * BLK
    half = n // 2
    dp = lax.axis_index("dp")
    me = lax.axis_index("seq")
    mx, my = me // ny, me % ny
    factor = HD ** (-0.5)

    def peer_of(o):
        return ((mx + o // ny) % nx) * ny + (my + o % ny) % ny

    barrier = pltpu.get_barrier_semaphore()

    def greet(o, c):
        pl.semaphore_signal(barrier, inc=1, device_id=(dp, peer_of(o)), device_id_type=MESH)
        return c

    def greet_dp(o, c):
        pl.semaphore_signal(barrier, inc=1, device_id=((dp + o) % ndp, me), device_id_type=MESH)
        return c

    lax.fori_loop(1, n, greet, 0)
    lax.fori_loop(1, ndp, greet_dp, 0)

    own_rows = pl.ds(pl.multiple_of(me * BLK, BLK), BLK)
    own_cols = pl.ds(pl.multiple_of(me * HD, HD), HD)
    ins = ((q_in, rq), (k_in, rk), (d_in, rd), (v_in, rv))

    def local_in(a):
        src, dst = ins[a]
        return pltpu.make_async_copy(src.at[0, :, own_cols], dst.at[own_rows, :], loc_sem.at[a])

    for a in range(4):
        local_in(a).start()
    meta_src[0:1, :] = seg_in[...]
    meta_src[1:2, :] = plan_in[...]
    meta[me] = meta_src[...]
    pl.semaphore_wait(barrier, n - 1 + ndp - 1)

    def send_meta(o):
        return pltpu.make_async_remote_copy(
            src_ref=meta_src, dst_ref=meta.at[me], send_sem=meta_send.at[o], recv_sem=meta_recv.at[o],
            device_id=(dp, peer_of(o)), device_id_type=MESH)

    def send_in(a, o):
        src, dst = ins[a]
        p = peer_of(o)
        return pltpu.make_async_remote_copy(
            src_ref=src.at[0, :, pl.ds(pl.multiple_of(p * HD, HD), HD)], dst_ref=dst.at[own_rows, :],
            send_sem=in_send.at[a, o], recv_sem=in_recv.at[a, o],
            device_id=(dp, p), device_id_type=MESH)

    def loop(lo, hi, body):
        def step(i, c):
            body(i)
            return c
        lax.fori_loop(lo, hi, step, 0)

    loop(1, n, lambda o: send_meta(o).start())
    for a in range(4):
        loop(1, n, lambda o, a=a: send_in(a, o).start())

    loop(1, n, lambda o: send_meta(o).wait())
    ids = meta[:, 0, :]
    starts = [jnp.int32(0)] + [jnp.sum((ids < c).astype(jnp.int32)) for c in (1, 2, 3)]
    ends = starts[1:] + [jnp.int32(length)]
    shift = jnp.int32(0)
    for lo, hi in zip(starts, ends):
        shift = shift + jnp.where(hi - lo == length // 2, lo, 0)

    lane = lax.broadcasted_iota(jnp.int32, (64, BLK), 1)
    sub = lax.broadcasted_iota(jnp.int32, (64, BLK), 0)

    def invert(d):
        row = jnp.zeros((1, BLK), jnp.int32)
        for g in range(BLK // 64):
            want = sub + (d * BLK + g * 64)
            acc = jnp.zeros((64, BLK), jnp.int32)
            for src in range(n):
                acc = jnp.maximum(acc, jnp.where(meta[src, 1:2, :] == want, lane + src * BLK, 0))
            col = jnp.max(acc, axis=1, keepdims=True)
            row = jnp.maximum(row, jnp.max(jnp.where(lane == sub + g * 64, col, 0), axis=0, keepdims=True))
        row = row - shift
        idx_v[d] = jnp.where(row < 0, row + length, row)

    loop(0, n, invert)
    to_smem = pltpu.make_async_copy(idx_v, idx_s, idx_sem)
    to_smem.start()

    def rotate_from(src):
        def conv(b):
            rows = pl.ds(pl.multiple_of(b * BLK, BLK), BLK)
            fbuf[rows, :] = src[rows, :].astype(jnp.float32)
        loop(0, n, conv)
        fbuf[length:length + BLK, :] = src[0:BLK, :].astype(jnp.float32)

    def offset(b):
        off = shift + b * BLK
        return jnp.where(off >= length, off - length, off)

    def arrive(a):
        local_in(a).wait()
        loop(1, n, lambda o: send_in(a, o).wait())

    wide_lane = lax.broadcasted_iota(jnp.int32, (BLK, HD), 1)
    wide_sub = lax.broadcasted_iota(jnp.int32, (BLK, HD), 0)

    def clip_of(off):
        pos = wide_sub + off
        pos = jnp.where(pos >= length, pos - length, pos)
        one = lambda b: jnp.where(pos >= b, 1, 0)
        return one(starts[1]) + one(starts[2]) + one(starts[3])

    def hat_of(x):
        rms = lax.rsqrt(rows_mean(x * x) + 1e-06)
        return x * rms, rms

    arrive(0)
    rotate_from(rq)

    def prep_q(b):
        off = offset(b)
        x = fbuf[pl.ds(off, BLK), :]
        raw_q[b] = x.astype(jnp.bfloat16)
        hat, _ = hat_of(x)
        qaug[b, :, 0:HD] = (hat * qg_in[...]).astype(jnp.bfloat16)
        qaug[b, :, HD:2 * HD] = jnp.where(wide_lane == clip_of(off), 1.0, 0.0).astype(jnp.bfloat16)

    loop(0, n, prep_q)

    arrive(1)
    rotate_from(rk)

    def prep_k(b):
        off = offset(b)
        x = fbuf[pl.ds(off, BLK), :]
        raw_k[b] = x.astype(jnp.bfloat16)
        hat, _ = hat_of(x)
        normed = (hat * kg_in[...]).astype(jnp.bfloat16)
        kaug[b, :, 0:HD] = normed
        other = jnp.where(wide_lane == clip_of(off), 0.0, jnp.where(wide_lane < 4, BIG, 0.0))
        kaug[b, :, HD:2 * HD] = other.astype(jnp.bfloat16)
        k_t[b] = normed.astype(jnp.float32).T.astype(jnp.bfloat16)

    loop(0, n, prep_k)

    scale = factor * LOG2E

    def weigh(t):
        first = (t // half) * half
        queries = qaug[t]
        top = None
        for c in range(half):
            s = lax.dot_general(kaug[first + c], queries, NT, preferred_element_type=jnp.float32)
            wbuf[t, c * BLK:(c + 1) * BLK, :] = s
            m = jnp.max(fold(s), axis=0)
            top = m if top is None else jnp.maximum(top, m)
        top = jnp.max(top, axis=0, keepdims=True) * scale
        total = jnp.zeros((8, BLK), jnp.float32)
        for c in range(half):
            w = jnp.exp2(wbuf[t, c * BLK:(c + 1) * BLK, :] * scale - top)
            wbuf[t, c * BLK:(c + 1) * BLK, :] = w
            total = total + jnp.sum(fold(w), axis=0)
        inv_ref[t] = 1.0 / jnp.sum(total, axis=0, keepdims=True)

    loop(0, n, weigh)

    arrive(2)
    rotate_from(rd)

    def prep_d(b):
        dor[b] = fbuf[pl.ds(offset(b), BLK), :].astype(jnp.bfloat16)

    loop(0, n, prep_d)

    def value_grad(b):
        first = (b // half) * half
        keys = pl.ds(pl.multiple_of((b - first) * BLK, BLK), BLK)
        acc = jnp.zeros((BLK, HD), jnp.float32)
        for t in range(half):
            probs = (wbuf[first + t, keys, :] * inv_ref[first + t]).astype(jnp.bfloat16)
            acc = acc + jnp.dot(probs, dor[first + t], preferred_element_type=jnp.float32)
        dvf[pl.ds(pl.multiple_of(b * BLK, BLK), BLK), :] = acc

    loop(0, n, value_grad)
    to_smem.wait()

    outs = ((rq, ov), (rk, oq), (rd, ok))

    def chunk(p):
        return pl.ds(pl.multiple_of(p * BLK, BLK), BLK)

    def send_out(a, o):
        src, dst = outs[a]
        p = peer_of(o)
        return pltpu.make_async_remote_copy(
            src_ref=src.at[chunk(p), :], dst_ref=dst.at[0, :, own_cols],
            send_sem=out_send.at[a, o], recv_sem=out_recv.at[a, o],
            device_id=(dp, p), device_id_type=MESH)

    def local_out(a):
        src, dst = outs[a]
        return pltpu.make_async_copy(src.at[own_rows, :], dst.at[0, :, own_cols], oloc_sem.at[a])

    def pick_v(p):
        def some(g):
            for u in range(16):
                j = g * 16 + u
                stage[pl.ds(j, 1), :] = dvf[pl.ds(idx_s[p, 0, j], 1), :]
        loop(0, BLK // 16, some)
        rq[chunk(p), :] = stage[...].astype(jnp.bfloat16)

    def out_v(o):
        pick_v(peer_of(o))
        send_out(0, o).start()

    loop(1, n, out_v)
    pick_v(me)
    local_out(0).start()

    arrive(3)
    rotate_from(rv)

    def prep_v(b):
        vr[b] = fbuf[pl.ds(offset(b), BLK), :].astype(jnp.bfloat16)
        dkf[b] = jnp.zeros((BLK, HD), jnp.float32)

    loop(0, n, prep_v)
    gpart[...] = jnp.zeros_like(gpart)

    def denorm(d_norm, raw, gain, row):
        hat, rms = hat_of(raw.astype(jnp.float32))
        gpart[row:row + 1, :] += jnp.sum(d_norm * hat, axis=0, keepdims=True)
        d_hat = d_norm * gain
        return rms * (d_hat - hat * rows_mean(d_hat * hat))

    def score_grad(t):
        first = (t // half) * half
        douts = dor[t]
        acc = jnp.zeros((8, BLK), jnp.float32)
        for c in range(half):
            d = lax.dot_general(vr[first + c], douts, NT, preferred_element_type=jnp.float32)
            dp_ref[c * BLK:(c + 1) * BLK, :] = d
            acc = acc + jnp.sum(fold(d * wbuf[t, c * BLK:(c + 1) * BLK, :]), axis=0)
        delta = jnp.sum(acc, axis=0, keepdims=True) * inv_ref[t]
        scaled = inv_ref[t] * factor
        queries = qaug[t, :, 0:HD]
        dq_t = jnp.zeros((HD, BLK), jnp.float32)
        for c in range(half):
            rows = slice(c * BLK, (c + 1) * BLK)
            ds = ((wbuf[t, rows, :] * scaled) * (dp_ref[rows, :] - delta)).astype(jnp.bfloat16)
            dkf[first + c] += jnp.dot(ds, queries, preferred_element_type=jnp.float32)
            dq_t = dq_t + jnp.dot(k_t[first + c], ds, preferred_element_type=jnp.float32)
        pair[pl.ds(t * (2 * BLK), BLK, stride=2), :] = denorm(dq_t.T, raw_q[t], qg_in[...], 0)

    loop(0, n, score_grad)

    def key_grad(b):
        pair[pl.ds(b * (2 * BLK) + 1, BLK, stride=2), :] = denorm(dkf[b], raw_k[b], kg_in[...], 1)

    loop(0, n, key_grad)

    gbuf1[me] = gpart[...]

    def send_g1(o):
        return pltpu.make_async_remote_copy(
            src_ref=gpart, dst_ref=gbuf1.at[me], send_sem=g1_send.at[o], recv_sem=g1_recv.at[o],
            device_id=(dp, peer_of(o)), device_id_type=MESH)

    def send_g2(o):
        return pltpu.make_async_remote_copy(
            src_ref=gsum, dst_ref=gbuf2.at[dp], send_sem=g2_send.at[o], recv_sem=g2_recv.at[o],
            device_id=((dp + o) % ndp, me), device_id_type=MESH)

    loop(1, n, lambda o: send_g1(o).start())
    loop(1, n, lambda o: send_out(0, o).wait_send())

    def pick_qk(p):
        def some(g):
            for u in range(16):
                j = g * 16 + u
                stage2[pl.ds(2 * j, 2), :] = pair[pl.ds(2 * idx_s[p, 0, j], 2), :]
        loop(0, BLK // 16, some)
        rk[chunk(p), :] = stage2[pl.ds(0, BLK, stride=2), :].astype(jnp.bfloat16)
        rd[chunk(p), :] = stage2[pl.ds(1, BLK, stride=2), :].astype(jnp.bfloat16)

    def out_qk(o):
        pick_qk(peer_of(o))
        send_out(1, o).start()
        send_out(2, o).start()

    loop(1, n, out_qk)
    pick_qk(me)
    local_out(1).start()
    local_out(2).start()

    loop(1, n, lambda o: send_g1(o).wait())
    gsum[...] = jnp.sum(gbuf1[...], axis=0)
    gbuf2[dp] = gsum[...]
    loop(1, ndp, lambda o: send_g2(o).start())
    loop(1, ndp, lambda o: send_g2(o).wait())
    grads = jnp.sum(gbuf2[...], axis=0)
    gq_out[...] = grads[0:1, :]
    gk_out[...] = grads[1:2, :]

    loop(1, n, lambda o: send_out(0, o).wait_recv())
    for a in (1, 2):
        loop(1, n, lambda o, a=a: send_out(a, o).wait())
    for a in range(3):
        local_out(a).wait()


def on_device(nx, ny, ndp, q_raw, k_raw, values, grad_out, segment_ids, row_plan, q_gain, k_gain):
    n = nx * ny
    length = n * BLK
    bf, f32, i32 = jnp.bfloat16, jnp.float32, jnp.int32
    dma = pltpu.SemaphoreType.DMA
    hbm = pl.BlockSpec(memory_space=pl.ANY)
    vmem = pl.BlockSpec(memory_space=pltpu.VMEM)
    big = jax.ShapeDtypeStruct(q_raw.shape, bf)
    small = jax.ShapeDtypeStruct((1, HD), f32)
    half = n // 2
    oq, ok, ov, gq, gk = pl.pallas_call(
        functools.partial(kernel, nx, ny, ndp),
        out_shape=(big, big, big, small, small),
        in_specs=[hbm] * 4 + [vmem] * 4,
        out_specs=(hbm, hbm, hbm, vmem, vmem),
        scratch_shapes=[
            pltpu.VMEM((length, HD), bf),
            pltpu.VMEM((length, HD), bf),
            pltpu.VMEM((length, HD), bf),
            pltpu.VMEM((length, HD), bf),
            pltpu.VMEM((2, BLK), i32),
            pltpu.VMEM((n, 2, BLK), i32),
            pltpu.VMEM((length + BLK, HD), f32),
            pltpu.VMEM((n, BLK, HD), bf),
            pltpu.VMEM((n, BLK, HD), bf),
            pltpu.VMEM((n, BLK, 2 * HD), bf),
            pltpu.VMEM((n, BLK, 2 * HD), bf),
            pltpu.VMEM((n, HD, BLK), bf),
            pltpu.VMEM((n, BLK, HD), bf),
            pltpu.VMEM((n, BLK, HD), bf),
            pltpu.VMEM((n, length // 2, BLK), f32),
            pltpu.VMEM((n, 1, BLK), f32),
            pltpu.VMEM((length // 2, BLK), f32),
            pltpu.VMEM((length, HD), f32),
            pltpu.VMEM((n, BLK, HD), f32),
            pltpu.VMEM((2 * length, HD), f32),
            pltpu.VMEM((BLK, HD), f32),
            pltpu.VMEM((2 * BLK, HD), f32),
            pltpu.VMEM((n, 1, BLK), i32),
            pltpu.SMEM((n, 1, BLK), i32),
            pltpu.VMEM((2, HD), f32),
            pltpu.VMEM((2, HD), f32),
            pltpu.VMEM((n, 2, HD), f32),
            pltpu.VMEM((ndp, 2, HD), f32),
            dma((4, n)), dma((4, n)), dma((n,)), dma((n,)), dma((3, n)), dma((3, n)),
            dma((n,)), dma((n,)), dma((ndp,)), dma((ndp,)), dma((4,)), dma((3,)), dma,
        ],
        compiler_params=pltpu.CompilerParams(
            collective_id=0, has_side_effects=True, vmem_limit_bytes=62 * 2**20),
        cost_estimate=pl.CostEstimate(
            flops=10 * HD * length * length // 2, bytes_accessed=14 * length * HD, transcendentals=length * length // 2),
        name="attention_backward",
    )(q_raw, k_raw, grad_out, values, segment_ids, row_plan, q_gain.reshape(1, HD), k_gain.reshape(1, HD))
    return oq, ok, ov, gq.reshape(HD), gk.reshape(HD)


def solution(mesh):
    rows = P("dp", "seq", None)
    n = mesh.shape["seq"]
    ny = 4
    return jax.shard_map(
        functools.partial(on_device, n // ny, ny, mesh.shape["dp"]),
        mesh=mesh,
        in_specs=(rows, rows, rows, rows, P("dp", "seq"), P("dp", "seq"), P(), P()),
        out_specs=(rows, rows, rows, P(), P()),
        check_vma=False,
    )
```

time: 770 us -> 143 us (0.19); the launches traced: 759 us -> 140 us
  other arithmetic: 229 us -> 0 us
  local copies, waits for them, and re-layouts: 185 us -> 6.16 us
  matrix products: 165 us -> 0 us
  Pallas kernels: 0 us -> 134 us
  blocking collectives: 123 us -> 0 us
  starting transfers between devices: 44.2 us -> 0 us
  loops' own time: 10.3 us -> 0 us
    dot_general x20 -> x0, matrix products: 165 us -> none  [the longest x4 73.1 us: step(): d_probs = jnp.dot(d_block, value_rows.T, preferred_element_type=jnp.float32)]
    pallas_call x0 -> x1, Pallas kernels: none -> 134 us  [on_device(): pl.pallas_call(functools.partial(kernel, nx, ny, ndp), out_shape=(big, bi...]
    unnamed x12 -> x0, other arithmetic: 117 us -> none
    psum x1 -> x0, blocking collectives: 87.7 us -> none  [on_device(): gain_q, gain_k = lax.psum((gain_q_part, gain_k_part), ('dp', 'seq'))]
    convert_element_type x11 -> x0, other arithmetic: 78 us -> none  [the longest x4 60.9 us: step(): d_scores = (probs * (d_probs - delta) * factor).astype(jnp.bfloat16)]
    gather x6 -> x0, local copies, waits for them, and re-layouts: 75.9 us -> none  [on_device(): pieces = tuple((item[:, inverse] for item in pieces))]
    unnamed x64 -> x13, local copies, waits for them, and re-layouts: 75.4 us -> 6.16 us
    all_to_all x7 -> x0, starting transfers between devices: 44.2 us -> none  [the longest x3 20.3 us: on_device(): lax.all_to_all(shortened(pieces), 'seq', split_axis=1, concat_axis=2, til...]
  transfers between devices with their start and end apart: 7 -> 0, of which waited for: 1 -> 0; matrix products, arithmetic and copies ran while one was open for 32% -> 0% of each run, Pallas kernels for 0% -> 0%
where the time goes in v1:
time: 143 us; the launch traced here: 140 us
  Pallas kernels  134 us (94%)
  local copies, waits for them, and re-layouts  6.16 us (4%)
    pallas_call x1, Pallas kernels, on_device(): pl.pallas_call(functools.partial(kernel, nx, ny, ndp), out_shape=(big, bi...  134 us
    unnamed x13, local copies, waits for them, and re-layouts  6.16 us

profile of v1, /device:TPU:1, one launch (start us, length us, event | category | flops | bytes accessed | tf_op | source)
XLA Modules:
  0.0 140.5 jit_solution(1791899628191595657)
XLA Ops:
  0.6 133.6 %attention_backward.1 = (bf16[1,256,2048]{2,1,0:T(8,128)(2,1)}, bf16[1,256,2048]{2,1,0:T(8,128)(2,1)}, bf16[1,256,2048]{2,1,0:T(8,128)(2,1)}, f32[1,128]{1,0:T(1,128)}, f32[1,128]{1,0:T(1,128)}) custom-call(bf16[1,256,2048]{2,1,0:T(8,128)(2,1)} %q_in.1, bf16[1,256,2048]{2,1,0:T(8,128)(2,1)} %k_in.1, bf16[1,256,2048]{2,1,0:T(8,128)(2,1)} %d_in.1, ...), custom_call_target="tpu_custom_call" | custom-call | flops 10737418240 | bytes 7340032 | tf_op jit(solution)/shard_map/attention_backward/pallas_call | solution.py:358
  134.3 0.0 copy-start.1
  134.3 2.4 %copy.18 = bf16[1,256,2048]{2,1,0:T(8,128)(2,1)} copy(bf16[1,256,2048]{2,1,0:T(8,128)(2,1)} %get-tuple-element.20) | data formatting | bytes 2097152
  136.7 0.0 copy-done.1
  136.7 0.0 copy-start
  136.7 1.0 copy.19
  137.7 0.6 copy-done
  138.3 0.0 copy-start.3
  138.3 1.0 copy.20
  139.3 0.0 copy-done.3
  139.3 0.0 copy-start.2
  139.3 0.5 copy.21
  139.8 0.2 copy-done.2
  139.9 0.5 copy.22
Async XLA Ops:
  134.3 2.4 %copy-start.1 = (bf16[1,256,2048]{2,1,0:T(8,128)(2,1)S(1)}, bf16[1,256,2048]{2,1,0:T(8,128)(2,1)}, u32[]{:S(2)}) copy-start(bf16[1,256,2048]{2,1,0:T(8,128)(2,1)} %get-tuple-element.21) | copy-start | bytes 3145732
  136.7 1.6 %copy-start = (bf16[1,256,2048]{2,1,0:T(8,128)(2,1)S(1)}, bf16[1,256,2048]{2,1,0:T(8,128)(2,1)}, u32[]{:S(2)}) copy-start(bf16[1,256,2048]{2,1,0:T(8,128)(2,1)} %get-tuple-element.22) | copy-start | bytes 3145732
  138.3 1.0 copy-start.3
  139.3 0.7 copy-start.2

commit v2 on v1

v2 whole, which is shorter than its diff:
```python
import functools
import jax
import jax.numpy as jnp
from jax import lax
from jax.experimental import pallas as pl
from jax.experimental.pallas import tpu as pltpu
from jax.sharding import PartitionSpec as P

HD = 128
BLK = 256
BIG = -1e30
LOG2E = 1.4426950408889634
MESH = pl.DeviceIdType.MESH
NT = (((1,), (1,)), ((), ()))


def rows_mean(x):
    return jnp.sum(x, axis=1, keepdims=True) * (1.0 / HD)


def fold(x):
    return x.reshape(x.shape[0] // 8, 8, x.shape[1])


def kernel(
    nx, ny, ndp,
    q_in, k_in, d_in, v_in, seg_in, plan_in, qg_in, kg_in,
    oq, ok, ov, gq_out, gk_out,
    rq, rk, rd, rv, meta_src, meta, fq, fk, fn,
    qaug, kaug, k_t, dor, vr,
    wbuf, inv_ref, dp_a, dp_b, dvf, dkf, stage,
    idx_v, idx_s, gpart, gsum, gbuf1, gbuf2,
    in_send, in_recv, meta_send, meta_recv, out_send, out_recv,
    g1_send, g1_recv, g2_send, g2_recv, loc_sem, oloc_sem, idx_sem,
):
    n = nx * ny
    length = n * BLK
    half = n // 2
    dp = lax.axis_index("dp")
    me = lax.axis_index("seq")
    mx, my = me // ny, me % ny
    factor = HD ** (-0.5)

    def peer_of(o):
        return ((mx + nx - o // ny) % nx) * ny + (my + ny - o % ny) % ny

    def source_of(o):
        return ((mx + o // ny) % nx) * ny + (my + o % ny) % ny

    barrier = pltpu.get_barrier_semaphore()

    def greet(o, c):
        pl.semaphore_signal(barrier, inc=1, device_id=(dp, peer_of(o)), device_id_type=MESH)
        return c

    def greet_dp(o, c):
        pl.semaphore_signal(barrier, inc=1, device_id=((dp + o) % ndp, me), device_id_type=MESH)
        return c

    lax.fori_loop(1, n, greet, 0)
    lax.fori_loop(1, ndp, greet_dp, 0)

    own_rows = pl.ds(pl.multiple_of(me * BLK, BLK), BLK)
    own_cols = pl.ds(pl.multiple_of(me * HD, HD), HD)
    ins = ((k_in, rk), (q_in, rq), (d_in, rd), (v_in, rv))

    def chunk(p):
        return pl.ds(pl.multiple_of(p * BLK, BLK), BLK)

    def local_in(a):
        src, dst = ins[a]
        return pltpu.make_async_copy(src.at[0, :, own_cols], dst.at[own_rows, :], loc_sem.at[a])

    for a in range(4):
        local_in(a).start()
    meta_src[0:1, :] = seg_in[...]
    meta_src[1:2, :] = plan_in[...]
    meta[me] = meta_src[...]
    pl.semaphore_wait(barrier, n - 1 + ndp - 1)

    def send_meta(o):
        return pltpu.make_async_remote_copy(
            src_ref=meta_src, dst_ref=meta.at[me], send_sem=meta_send.at[o], recv_sem=meta_recv.at[o],
            device_id=(dp, peer_of(o)), device_id_type=MESH)

    def send_in(a, o):
        src, dst = ins[a]
        p = peer_of(o)
        return pltpu.make_async_remote_copy(
            src_ref=src.at[0, :, pl.ds(pl.multiple_of(p * HD, HD), HD)], dst_ref=dst.at[own_rows, :],
            send_sem=in_send.at[a, o], recv_sem=in_recv.at[a, o],
            device_id=(dp, p), device_id_type=MESH)

    def loop(lo, hi, body):
        def step(i, c):
            body(i)
            return c
        lax.fori_loop(lo, hi, step, 0)

    loop(1, n, lambda o: send_meta(o).start())
    for a in range(4):
        loop(1, n, lambda o, a=a: send_in(a, o).start())

    loop(1, n, lambda o: send_meta(o).wait())
    ids = meta[:, 0, :]
    starts = [jnp.int32(0)] + [jnp.sum((ids < c).astype(jnp.int32)) for c in (1, 2, 3)]
    ends = starts[1:] + [jnp.int32(length)]
    shift = jnp.int32(0)
    for lo, hi in zip(starts, ends):
        shift = shift + jnp.where(hi - lo == length // 2, lo, 0)

    slip = lax.rem(shift, BLK)
    lead = lax.div(shift, BLK)

    def kin(tile, c):
        outside = jnp.where(lax.rem(tile + n - lead, n) >= half, half, 0)
        return lax.rem(lead + outside + c, n)

    lane = lax.broadcasted_iota(jnp.int32, (64, BLK), 1)
    sub = lax.broadcasted_iota(jnp.int32, (64, BLK), 0)

    def invert(d):
        row = jnp.zeros((1, BLK), jnp.int32)
        for g in range(BLK // 64):
            want = sub + (d * BLK + g * 64)
            acc = jnp.zeros((64, BLK), jnp.int32)
            for src in range(n):
                acc = jnp.maximum(acc, jnp.where(meta[src, 1:2, :] == want, lane + src * BLK, 0))
            col = jnp.max(acc, axis=1, keepdims=True)
            row = jnp.maximum(row, jnp.max(jnp.where(lane == sub + g * 64, col, 0), axis=0, keepdims=True))
        row = row - slip
        idx_v[d] = jnp.where(row < 0, row + length, row)

    loop(0, n, invert)
    to_smem = pltpu.make_async_copy(idx_v, idx_s, idx_sem)
    to_smem.start()

    def on_arrival(a, take, tile):
        def get(o):
            send_in(a, o).wait_recv()
            p = source_of(o)
            take(p, p)

            @pl.when(p == 0)
            def _():
                take(0, n)

        local_in(a).wait()
        take(me, me)

        @pl.when(me == 0)
        def _():
            take(0, n)

        loop(1, ny, get)

        def one(k):
            @pl.when((k % ny == ny - 1) & (k < n - ny))
            def _():
                loop(k + 1, k + 1 + ny, get)
            tile(((mx + k // ny) % nx) * ny + k % ny)

        loop(0, n, one)

    def rows_of(u):
        return pl.ds(u * BLK + slip, BLK)

    wide_lane = lax.broadcasted_iota(jnp.int32, (BLK, HD), 1)
    wide_sub = lax.broadcasted_iota(jnp.int32, (BLK, HD), 0)

    def clip_of(u):
        pos = wide_sub + (slip + u * BLK)
        pos = jnp.where(pos >= length, pos - length, pos)
        one = lambda b: jnp.where(pos >= b, 1, 0)
        return one(starts[1]) + one(starts[2]) + one(starts[3])

    def hat_of(x):
        rms = lax.rsqrt(rows_mean(x * x) + 1e-06)
        return x * rms, rms

    def norm_chunk(src, full, gain, o, to):
        x = src[chunk(o), :].astype(jnp.float32)
        full[chunk(to), :] = x
        hat, _ = hat_of(x)
        fn[chunk(to), :] = (hat * gain[...]).astype(jnp.bfloat16).astype(jnp.float32)

    def prep_k(b):
        x = fn[rows_of(b), :]
        kaug[b, :, 0:HD] = x.astype(jnp.bfloat16)
        other = jnp.where(wide_lane == clip_of(b), 0.0, jnp.where(wide_lane < 4, BIG, 0.0))
        kaug[b, :, HD:2 * HD] = other.astype(jnp.bfloat16)
        k_t[b] = x.T.astype(jnp.bfloat16)

    on_arrival(0, lambda o, to: norm_chunk(rk, fk, kg_in, o, to), prep_k)

    def prep_q(b):
        qaug[b, :, 0:HD] = fn[rows_of(b), :].astype(jnp.bfloat16)
        qaug[b, :, HD:2 * HD] = jnp.where(wide_lane == clip_of(b), 1.0, 0.0).astype(jnp.bfloat16)

    scale = factor * LOG2E

    def weigh(t):
        queries = qaug[t]
        top = None
        for c in range(half):
            s = lax.dot_general(kaug[kin(t, c)], queries, NT, preferred_element_type=jnp.float32)
            wbuf[t, c] = s
            m = jnp.max(fold(s), axis=0)
            top = m if top is None else jnp.maximum(top, m)
        top = jnp.max(top, axis=0, keepdims=True) * scale
        total = jnp.zeros((8, BLK), jnp.float32)
        for c in range(half):
            w = jnp.exp2(wbuf[t, c] * scale - top)
            wbuf[t, c] = w
            total = total + jnp.sum(fold(w), axis=0)
        inv_ref[t] = 1.0 / jnp.sum(total, axis=0, keepdims=True)

    def take_q(b):
        prep_q(b)
        weigh(b)

    on_arrival(1, lambda o, to: norm_chunk(rq, fq, qg_in, o, to), take_q)

    def widen(src, o, to):
        fn[chunk(to), :] = src[chunk(o), :].astype(jnp.float32)

    def prep_d(b):
        dor[b] = fn[rows_of(b), :].astype(jnp.bfloat16)

    on_arrival(2, lambda o, to: widen(rd, o, to), prep_d)

    def place(b):
        return lax.rem(b + n - lead, half)

    def value_grad(b):
        acc = jnp.zeros((BLK, HD), jnp.float32)
        for j in range(half):
            t = kin(b, j)
            probs = (wbuf[t, place(b)] * inv_ref[t]).astype(jnp.bfloat16)
            acc = acc + jnp.dot(probs, dor[t], preferred_element_type=jnp.float32)
        dvf[chunk(b), :] = acc

    loop(0, n, value_grad)
    to_smem.wait()

    outs = ((rq, ov), (rk, oq), (rd, ok))

    def send_out(a, o):
        src, dst = outs[a]
        p = peer_of(o)
        return pltpu.make_async_remote_copy(
            src_ref=src.at[chunk(p), :], dst_ref=dst.at[0, :, own_cols],
            send_sem=out_send.at[a, o], recv_sem=out_recv.at[a, o],
            device_id=(dp, p), device_id_type=MESH)

    def local_out(a):
        src, dst = outs[a]
        return pltpu.make_async_copy(src.at[own_rows, :], dst.at[0, :, own_cols], oloc_sem.at[a])

    def pick(rows, a, p, lo, count):
        for j in range(lo, lo + count):
            stage[j:j + 1, :] = rows[pl.ds(idx_s[p, 0, j], 1), :]
        out = outs[a][0]
        out[pl.ds(pl.multiple_of(p * BLK + lo, 16), count), :] = stage[lo:lo + count, :].astype(jnp.bfloat16)

    def leave(a, o):
        @pl.when(o == 0)
        def _():
            local_out(a).start()

        @pl.when(o != 0)
        def _():
            send_out(a, o).start()

    def prep_v(b):
        vr[b] = fn[rows_of(b), :].astype(jnp.bfloat16)

    on_arrival(3, lambda o, to: widen(rv, o, to), prep_v)
    gpart[...] = jnp.zeros_like(gpart)

    def denorm(rows, full, b, gain, row):
        hat, rms = hat_of(full[rows_of(b), :])
        d_norm = rows[chunk(b), :]
        gpart[row:row + 1, :] += jnp.sum(d_norm * hat, axis=0, keepdims=True)
        d_hat = d_norm * gain[...]
        rows[chunk(b), :] = rms * (d_hat - hat * rows_mean(d_hat * hat))

    part = BLK // half

    def value_dot(t, c):
        return lax.dot_general(vr[kin(t, c)], dor[t], NT, preferred_element_type=jnp.float32)

    def weighted(d, t, c):
        return jnp.sum(fold(d * wbuf[t, c]), axis=0)

    def score_grad(t, acc, now, t_next, later, last):
        dest = peer_of(t)
        delta = jnp.sum(acc, axis=0, keepdims=True) * inv_ref[t]
        scaled = inv_ref[t] * factor
        dq_t = jnp.zeros((HD, BLK), jnp.float32)
        acc = jnp.zeros((8, BLK), jnp.float32)
        for c in range(half):
            d = value_dot(t_next, c)
            ds = (wbuf[t, c] * scaled) * (now[c] - delta)
            wbuf[t, c] = ds
            dq_t = dq_t + jnp.dot(k_t[kin(t, c)], ds.astype(jnp.bfloat16), preferred_element_type=jnp.float32)
            later[c] = d
            acc = acc + weighted(d, t_next, c)
            pick(dvf, 0, dest, c * part, part)
        fn[chunk(t), :] = dq_t.T
        last()
        leave(0, t)
        return acc

    acc = jnp.zeros((8, BLK), jnp.float32)
    for c in range(half):
        d = value_dot(0, c)
        dp_a[c] = d
        acc = acc + weighted(d, 0, c)

    def two(i, acc):
        t = 2 * i
        acc = score_grad(t, acc, dp_a, t + 1, dp_b, lambda: None)
        return score_grad(t + 1, acc, dp_b, (t + 2) % n, dp_a, lambda: denorm(fn, fq, t, qg_in, 0))

    lax.fori_loop(0, n // 2, two, acc)
    loop(0, n // 2, lambda i: denorm(fn, fq, 2 * i + 1, qg_in, 0))

    def key_grad(b):
        dest = peer_of(b)
        acc = jnp.zeros((BLK, HD), jnp.float32)
        for j in range(half):
            t = kin(b, j)
            ds = wbuf[t, place(b)].astype(jnp.bfloat16)
            acc = acc + jnp.dot(ds, qaug[t, :, 0:HD], preferred_element_type=jnp.float32)
            pick(fn, 1, dest, j * part, part)
        dkf[chunk(b), :] = acc
        leave(1, b)

    loop(0, n, key_grad)
    loop(0, n, lambda b: denorm(dkf, fk, b, kg_in, 1))

    gbuf1[me] = gpart[...]

    def send_g1(o):
        return pltpu.make_async_remote_copy(
            src_ref=gpart, dst_ref=gbuf1.at[me], send_sem=g1_send.at[o], recv_sem=g1_recv.at[o],
            device_id=(dp, peer_of(o)), device_id_type=MESH)

    def send_g2(o):
        return pltpu.make_async_remote_copy(
            src_ref=gsum, dst_ref=gbuf2.at[dp], send_sem=g2_send.at[o], recv_sem=g2_recv.at[o],
            device_id=((dp + o) % ndp, me), device_id_type=MESH)

    loop(1, n, lambda o: send_g1(o).start())

    def key_rows(o):
        pick(dkf, 2, peer_of(o), 0, BLK)
        leave(2, o)

    loop(0, n // 4, key_rows)
    loop(1, n, lambda o: send_g1(o).wait())
    gsum[...] = jnp.sum(gbuf1[...], axis=0)
    gbuf2[dp] = gsum[...]
    loop(1, ndp, lambda o: send_g2(o).start())
    loop(n // 4, n, key_rows)

    loop(1, ndp, lambda o: send_g2(o).wait())
    grads = jnp.sum(gbuf2[...], axis=0)
    gq_out[...] = grads[0:1, :]
    gk_out[...] = grads[1:2, :]

    for a in range(4):
        loop(1, n, lambda o, a=a: send_in(a, o).wait_send())
    for a in range(3):
        loop(1, n, lambda o, a=a: send_out(a, o).wait())
    for a in range(3):
        local_out(a).wait()


def on_device(nx, ny, ndp, q_raw, k_raw, values, grad_out, segment_ids, row_plan, q_gain, k_gain):
    n = nx * ny
    length = n * BLK
    bf, f32, i32 = jnp.bfloat16, jnp.float32, jnp.int32
    dma = pltpu.SemaphoreType.DMA
    hbm = pl.BlockSpec(memory_space=pl.ANY)
    vmem = pl.BlockSpec(memory_space=pltpu.VMEM)
    big = jax.ShapeDtypeStruct(q_raw.shape, bf)
    small = jax.ShapeDtypeStruct((1, HD), f32)
    half = n // 2
    oq, ok, ov, gq, gk = pl.pallas_call(
        functools.partial(kernel, nx, ny, ndp),
        out_shape=(big, big, big, small, small),
        in_specs=[hbm] * 4 + [vmem] * 4,
        out_specs=(hbm, hbm, hbm, vmem, vmem),
        scratch_shapes=[
            pltpu.VMEM((length, HD), bf),
            pltpu.VMEM((length, HD), bf),
            pltpu.VMEM((length, HD), bf),
            pltpu.VMEM((length, HD), bf),
            pltpu.VMEM((2, BLK), i32),
            pltpu.VMEM((n, 2, BLK), i32),
            pltpu.VMEM((length + BLK, HD), f32),
            pltpu.VMEM((length + BLK, HD), f32),
            pltpu.VMEM((length + BLK, HD), f32),
            pltpu.VMEM((n, BLK, 2 * HD), bf),
            pltpu.VMEM((n, BLK, 2 * HD), bf),
            pltpu.VMEM((n, HD, BLK), bf),
            pltpu.VMEM((n, BLK, HD), bf),
            pltpu.VMEM((n, BLK, HD), bf),
            pltpu.VMEM((n, half, BLK, BLK), f32),
            pltpu.VMEM((n, 1, BLK), f32),
            pltpu.VMEM((half, BLK, BLK), f32),
            pltpu.VMEM((half, BLK, BLK), f32),
            pltpu.VMEM((length, HD), f32),
            pltpu.VMEM((length, HD), f32),
            pltpu.VMEM((BLK, HD), f32),
            pltpu.VMEM((n, 1, BLK), i32),
            pltpu.SMEM((n, 1, BLK), i32),
            pltpu.VMEM((2, HD), f32),
            pltpu.VMEM((2, HD), f32),
            pltpu.VMEM((n, 2, HD), f32),
            pltpu.VMEM((ndp, 2, HD), f32),
            dma((4, n)), dma((4, n)), dma((n,)), dma((n,)), dma((3, n)), dma((3, n)),
            dma((n,)), dma((n,)), dma((ndp,)), dma((ndp,)), dma((4,)), dma((3,)), dma,
        ],
        compiler_params=pltpu.CompilerParams(
            collective_id=0, has_side_effects=True, vmem_limit_bytes=62 * 2**20),
        cost_estimate=pl.CostEstimate(
            flops=10 * HD * length * length // 2, bytes_accessed=14 * length * HD, transcendentals=length * length // 2),
        name="attention_backward",
    )(q_raw, k_raw, grad_out, values, segment_ids, row_plan, q_gain.reshape(1, HD), k_gain.reshape(1, HD))
    return oq, ok, ov, gq.reshape(HD), gk.reshape(HD)


def solution(mesh):
    rows = P("dp", "seq", None)
    n = mesh.shape["seq"]
    ny = 4
    return jax.shard_map(
        functools.partial(on_device, n // ny, ny, mesh.shape["dp"]),
        mesh=mesh,
        in_specs=(rows, rows, rows, rows, P("dp", "seq"), P("dp", "seq"), P(), P()),
        out_specs=(rows, rows, rows, P(), P()),
        check_vma=False,
    )
```

time: 143 us -> 127 us (0.89); the launches traced: 140 us -> 126 us
  Pallas kernels: 134 us -> 119 us
    pallas_call x1, Pallas kernels: 134 us -> 119 us  [on_device(): pl.pallas_call(functools.partial(kernel, nx, ny, ndp), out_shape=(big, bi...]
where the time goes in v2:
time: 127 us; the launch traced here: 126 us
  Pallas kernels  119 us (94%)
  local copies, waits for them, and re-layouts  6.16 us (5%)
    pallas_call x1, Pallas kernels, on_device(): pl.pallas_call(functools.partial(kernel, nx, ny, ndp), out_shape=(big, bi...  119 us
    unnamed x13, local copies, waits for them, and re-layouts  6.16 us

profile of v2, /device:TPU:1, one launch (start us, length us, event | category | flops | bytes accessed | tf_op | source)
XLA Modules:
  0.0 126.3 jit_solution(4814334152417524332)
XLA Ops:
  0.6 119.5 %attention_backward.1 = (bf16[1,256,2048]{2,1,0:T(8,128)(2,1)}, bf16[1,256,2048]{2,1,0:T(8,128)(2,1)}, bf16[1,256,2048]{2,1,0:T(8,128)(2,1)}, f32[1,128]{1,0:T(1,128)}, f32[1,128]{1,0:T(1,128)}) custom-call(bf16[1,256,2048]{2,1,0:T(8,128)(2,1)} %q_in.1, bf16[1,256,2048]{2,1,0:T(8,128)(2,1)} %k_in.1, bf16[1,256,2048]{2,1,0:T(8,128)(2,1)} %d_in.1, ...), custom_call_target="tpu_custom_call" | custom-call | flops 10737418240 | bytes 7340032 | tf_op jit(solution)/shard_map/attention_backward/pallas_call | solution.py:391
  120.1 0.0 copy-start.1
  120.1 2.4 %copy.18 = bf16[1,256,2048]{2,1,0:T(8,128)(2,1)} copy(bf16[1,256,2048]{2,1,0:T(8,128)(2,1)} %get-tuple-element.20) | data formatting | bytes 2097152
  122.5 0.0 copy-done.1
  122.5 0.0 copy-start
  122.5 1.0 copy.19
  123.5 0.6 copy-done
  124.1 0.0 copy-start.3
  124.1 1.0 copy.20
  125.1 0.0 copy-done.3
  125.1 0.0 copy-start.2
  125.1 0.5 copy.21
  125.6 0.2 copy-done.2
  125.8 0.5 copy.22
Async XLA Ops:
  120.1 2.4 %copy-start.1 = (bf16[1,256,2048]{2,1,0:T(8,128)(2,1)S(1)}, bf16[1,256,2048]{2,1,0:T(8,128)(2,1)}, u32[]{:S(2)}) copy-start(bf16[1,256,2048]{2,1,0:T(8,128)(2,1)} %get-tuple-element.21) | copy-start | bytes 3145732
  122.5 1.6 %copy-start = (bf16[1,256,2048]{2,1,0:T(8,128)(2,1)S(1)}, bf16[1,256,2048]{2,1,0:T(8,128)(2,1)}, u32[]{:S(2)}) copy-start(bf16[1,256,2048]{2,1,0:T(8,128)(2,1)} %get-tuple-element.22) | copy-start | bytes 3145732
  124.1 1.0 copy-start.3
  125.1 0.7 copy-start.2

commit v3 on v2

--- a/solution.py
+++ b/solution.py
@@ -47,6 +47,12 @@
     def source_of(o):
         return ((mx + o // ny) % nx) * ny + (my + o % ny) % ny
 
+    def stride(o):
+        return (o * (5 + 6 * (dp % 2))) % n
+
+    def mixed(o):
+        return peer_of(stride(o))
+
     barrier = pltpu.get_barrier_semaphore()
 
     def greet(o, c):
@@ -99,7 +105,7 @@
 
     loop(1, n, lambda o: send_meta(o).start())
     for a in range(4):
-        loop(1, n, lambda o, a=a: send_in(a, o).start())
+        loop(1, n, lambda o, a=a: send_in(a, stride(o)).start())
 
     loop(1, n, lambda o: send_meta(o).wait())
     ids = meta[:, 0, :]
@@ -158,7 +164,7 @@
             @pl.when((k % ny == ny - 1) & (k < n - ny))
             def _():
                 loop(k + 1, k + 1 + ny, get)
-            tile(((mx + k // ny) % nx) * ny + k % ny)
+            tile(((mx + k // ny) % nx) * ny + k % ny, k)
 
         loop(0, n, one)
 
@@ -191,7 +197,7 @@
         kaug[b, :, HD:2 * HD] = other.astype(jnp.bfloat16)
         k_t[b] = x.T.astype(jnp.bfloat16)
 
-    on_arrival(0, lambda o, to: norm_chunk(rk, fk, kg_in, o, to), prep_k)
+    on_arrival(0, lambda o, to: norm_chunk(rk, fk, kg_in, o, to), lambda b, k: prep_k(b))
 
     def prep_q(b):
         qaug[b, :, 0:HD] = fn[rows_of(b), :].astype(jnp.bfloat16)
@@ -215,7 +221,7 @@
             total = total + jnp.sum(fold(w), axis=0)
         inv_ref[t] = 1.0 / jnp.sum(total, axis=0, keepdims=True)
 
-    def take_q(b):
+    def take_q(b, k):
         prep_q(b)
         weigh(b)
 
@@ -227,7 +233,7 @@
     def prep_d(b):
         dor[b] = fn[rows_of(b), :].astype(jnp.bfloat16)
 
-    on_arrival(2, lambda o, to: widen(rd, o, to), prep_d)
+    on_arrival(2, lambda o, to: widen(rd, o, to), lambda b, k: prep_d(b))
 
     def place(b):
         return lax.rem(b + n - lead, half)
@@ -247,7 +253,7 @@
 
     def send_out(a, o):
         src, dst = outs[a]
-        p = peer_of(o)
+        p = mixed(o)
         return pltpu.make_async_remote_copy(
             src_ref=src.at[chunk(p), :], dst_ref=dst.at[0, :, own_cols],
             send_sem=out_send.at[a, o], recv_sem=out_recv.at[a, o],
@@ -272,18 +278,26 @@
         def _():
             send_out(a, o).start()
 
-    def prep_v(b):
+    def take_v(b, k):
         vr[b] = fn[rows_of(b), :].astype(jnp.bfloat16)
-
-    on_arrival(3, lambda o, to: widen(rv, o, to), prep_v)
+        pick(dvf, 0, mixed(k), 0, BLK)
+        leave(0, k)
+
+    on_arrival(3, lambda o, to: widen(rv, o, to), take_v)
     gpart[...] = jnp.zeros_like(gpart)
 
-    def denorm(rows, full, b, gain, row):
+    def denorm(rows, full, b, gain):
         hat, rms = hat_of(full[rows_of(b), :])
         d_norm = rows[chunk(b), :]
-        gpart[row:row + 1, :] += jnp.sum(d_norm * hat, axis=0, keepdims=True)
         d_hat = d_norm * gain[...]
         rows[chunk(b), :] = rms * (d_hat - hat * rows_mean(d_hat * hat))
+        return d_norm, hat
+
+    def denorm_q(b, valid=True):
+        d_norm, hat = denorm(fn, fq, b, qg_in)
+        normed = qaug[b, :, 0:HD].astype(jnp.float32)
+        gpart[0:1, :] += jnp.where(valid, jnp.sum(d_norm * hat, axis=0, keepdims=True), 0.0)
+        gpart[1:2, :] += jnp.where(valid, jnp.sum(d_norm * normed, axis=0, keepdims=True), 0.0)
 
     part = BLK // half
 
@@ -293,8 +307,8 @@
     def weighted(d, t, c):
         return jnp.sum(fold(d * wbuf[t, c]), axis=0)
 
-    def score_grad(t, acc, now, t_next, later, last):
-        dest = peer_of(t)
+    def score_grad(t, acc, now, t_next, later):
+        denorm_q((t + n - 1) % n, t > 0)
         delta = jnp.sum(acc, axis=0, keepdims=True) * inv_ref[t]
         scaled = inv_ref[t] * factor
         dq_t = jnp.zeros((HD, BLK), jnp.float32)
@@ -306,10 +320,7 @@
             dq_t = dq_t + jnp.dot(k_t[kin(t, c)], ds.astype(jnp.bfloat16), preferred_element_type=jnp.float32)
             later[c] = d
             acc = acc + weighted(d, t_next, c)
-            pick(dvf, 0, dest, c * part, part)
         fn[chunk(t), :] = dq_t.T
-        last()
-        leave(0, t)
         return acc
 
     acc = jnp.zeros((8, BLK), jnp.float32)
@@ -320,14 +331,31 @@
 
     def two(i, acc):
         t = 2 * i
-        acc = score_grad(t, acc, dp_a, t + 1, dp_b, lambda: None)
-        return score_grad(t + 1, acc, dp_b, (t + 2) % n, dp_a, lambda: denorm(fn, fq, t, qg_in, 0))
+        acc = score_grad(t, acc, dp_a, t + 1, dp_b)
+        return score_grad(t + 1, acc, dp_b, (t + 2) % n, dp_a)
 
     lax.fori_loop(0, n // 2, two, acc)
-    loop(0, n // 2, lambda i: denorm(fn, fq, 2 * i + 1, qg_in, 0))
+    denorm_q(n - 1)
+    gpart[1:2, :] = gpart[1:2, :] / kg_in[...]
+    dkf[chunk(n - 1), :] = jnp.zeros((BLK, HD), jnp.float32)
+
+    gbuf1[me] = gpart[...]
+
+    def send_g1(o):
+        return pltpu.make_async_remote_copy(
+            src_ref=gpart, dst_ref=gbuf1.at[me], send_sem=g1_send.at[o], recv_sem=g1_recv.at[o],
+            device_id=(dp, peer_of(o)), device_id_type=MESH)
+
+    def send_g2(o):
+        return pltpu.make_async_remote_copy(
+            src_ref=gsum, dst_ref=gbuf2.at[dp], send_sem=g2_send.at[o], recv_sem=g2_recv.at[o],
+            device_id=((dp + o) % ndp, me), device_id_type=MESH)
+
+    loop(1, n, lambda o: send_g1(o).start())
 
     def key_grad(b):
-        dest = peer_of(b)
+        dest = mixed(b)
+        denorm(dkf, fk, (b + n - 1) % n, kg_in)
         acc = jnp.zeros((BLK, HD), jnp.float32)
         for j in range(half):
             t = kin(b, j)
@@ -338,32 +366,17 @@
         leave(1, b)
 
     loop(0, n, key_grad)
-    loop(0, n, lambda b: denorm(dkf, fk, b, kg_in, 1))
-
-    gbuf1[me] = gpart[...]
-
-    def send_g1(o):
-        return pltpu.make_async_remote_copy(
-            src_ref=gpart, dst_ref=gbuf1.at[me], send_sem=g1_send.at[o], recv_sem=g1_recv.at[o],
-            device_id=(dp, peer_of(o)), device_id_type=MESH)
-
-    def send_g2(o):
-        return pltpu.make_async_remote_copy(
-            src_ref=gsum, dst_ref=gbuf2.at[dp], send_sem=g2_send.at[o], recv_sem=g2_recv.at[o],
-            device_id=((dp + o) % ndp, me), device_id_type=MESH)
-
-    loop(1, n, lambda o: send_g1(o).start())
+    denorm(dkf, fk, n - 1, kg_in)
 
     def key_rows(o):
-        pick(dkf, 2, peer_of(o), 0, BLK)
+        pick(dkf, 2, mixed(o), 0, BLK)
         leave(2, o)
 
-    loop(0, n // 4, key_rows)
     loop(1, n, lambda o: send_g1(o).wait())
     gsum[...] = jnp.sum(gbuf1[...], axis=0)
     gbuf2[dp] = gsum[...]
     loop(1, ndp, lambda o: send_g2(o).start())
-    loop(n // 4, n, key_rows)
+    loop(0, n, key_rows)
 
     loop(1, ndp, lambda o: send_g2(o).wait())
     grads = jnp.sum(gbuf2[...], axis=0)
@@ -376,6 +389,29 @@
         loop(1, n, lambda o, a=a: send_out(a, o).wait())
     for a in range(3):
         local_out(a).wait()
+
+
+def hand_over(q, k, v, gq, gk, oq, ok, ov, gq_out, gk_out, held, sem):
+    pairs = ((q, oq), (k, ok), (v, ov))
+    parts = 2
+    size = q.shape[1] // parts
+
+    def move(a, part):
+        rows = pl.ds(part * size, size)
+        src, dst = pairs[a]
+        return (pltpu.make_async_copy(src.at[0, rows, :], held.at[a, rows, :], sem.at[0, a, part]),
+                pltpu.make_async_copy(held.at[a, rows, :], dst.at[0, rows, :], sem.at[1, a, part]))
+
+    moves = [move(a, part) for a in range(3) for part in range(parts)]
+    for get, _ in moves:
+        get.start()
+    gq_out[...] = gq[...]
+    gk_out[...] = gk[...]
+    for get, put in moves:
+        get.wait()
+        put.start()
+    for _, put in moves:
+        put.wait()
 
 
 def on_device(nx, ny, ndp, q_raw, k_raw, values, grad_out, segment_ids, row_plan, q_gain, k_gain):
@@ -430,6 +466,14 @@
             flops=10 * HD * length * length // 2, bytes_accessed=14 * length * HD, transcendentals=length * length // 2),
         name="attention_backward",
     )(q_raw, k_raw, grad_out, values, segment_ids, row_plan, q_gain.reshape(1, HD), k_gain.reshape(1, HD))
+    oq, ok, ov, gq, gk = pl.pallas_call(
+        hand_over,
+        out_shape=(big, big, big, small, small),
+        in_specs=[hbm] * 3 + [vmem] * 2,
+        out_specs=(hbm, hbm, hbm, vmem, vmem),
+        scratch_shapes=[pltpu.VMEM((3,) + q_raw.shape[1:], bf), dma((2, 3, 2))],
+        name="hand_over",
+    )(oq, ok, ov, gq, gk)
     return oq, ok, ov, gq.reshape(HD), gk.reshape(HD)
 
 

time: 127 us -> 114 us (0.90)
  local copies, waits for them, and re-layouts: 6.16 us -> 0 us
  Pallas kernels: 119 us -> 113 us
    pallas_call x1, Pallas kernels: 119 us -> 109 us  [on_device(): pl.pallas_call(functools.partial(kernel, nx, ny, ndp), out_shape=(big, bi...]
    unnamed x13 -> x0, local copies, waits for them, and re-layouts: 6.16 us -> none
    pallas_call x0 -> x1, Pallas kernels: none -> 4 us  [on_device(): pl.pallas_call(hand_over, out_shape=(big, big, big, small, small), in_spe...]
where the time goes in v3:
time: 114 us; the launch traced here: 113 us
  Pallas kernels  113 us (99%)
    pallas_call x1, Pallas kernels, on_device(): pl.pallas_call(functools.partial(kernel, nx, ny, ndp), out_shape=(big, bi...  109 us
    pallas_call x1, Pallas kernels, on_device(): pl.pallas_call(hand_over, out_shape=(big, big, big, small, small), in_spe...  4 us

profile of v3, /device:TPU:1, one launch (start us, length us, event | category | flops | bytes accessed | tf_op | source)
XLA Modules:
  0.0 113.4 jit_solution(5332298710327600160)
XLA Ops:
  0.6 108.8 %attention_backward.1 = (bf16[1,256,2048]{2,1,0:T(8,128)(2,1)}, bf16[1,256,2048]{2,1,0:T(8,128)(2,1)}, bf16[1,256,2048]{2,1,0:T(8,128)(2,1)}, f32[1,128]{1,0:T(1,128)}, f32[1,128]{1,0:T(1,128)}) custom-call(bf16[1,256,2048]{2,1,0:T(8,128)(2,1)} %q_in.1, bf16[1,256,2048]{2,1,0:T(8,128)(2,1)} %k_in.1, bf16[1,256,2048]{2,1,0:T(8,128)(2,1)} %d_in.1, ...), custom_call_target="tpu_custom_call" | custom-call | flops 10737418240 | bytes 7340032 | tf_op jit(solution)/shard_map/attention_backward/pallas_call | solution.py:427
  109.4 4.0 %hand_over.1 = (bf16[1,256,2048]{2,1,0:T(8,128)(2,1)}, bf16[1,256,2048]{2,1,0:T(8,128)(2,1)}, bf16[1,256,2048]{2,1,0:T(8,128)(2,1)}, f32[1,128]{1,0:T(1,128)}, f32[1,128]{1,0:T(1,128)}) custom-call(bf16[1,256,2048]{2,1,0:T(8,128)(2,1)} %get-tuple-element.15.q, bf16[1,256,2048]{2,1,0:T(8,128)(2,1)} %get-tuple-element.16.k, ...), custom_call_target="tpu_custom_call" | custom-call | tf_op jit(solution)/shard_map/hand_over/pallas_call | solution.py:469

commit v4 on v3

--- a/solution.py
+++ b/solution.py
@@ -48,7 +48,7 @@
         return ((mx + o // ny) % nx) * ny + (my + o % ny) % ny
 
     def stride(o):
-        return (o * (5 + 6 * (dp % 2))) % n
+        return (o * (7 + 2 * (dp % 2))) % n
 
     def mixed(o):
         return peer_of(stride(o))
@@ -393,7 +393,7 @@
 
 def hand_over(q, k, v, gq, gk, oq, ok, ov, gq_out, gk_out, held, sem):
     pairs = ((q, oq), (k, ok), (v, ov))
-    parts = 2
+    parts = 4
     size = q.shape[1] // parts
 
     def move(a, part):
@@ -471,7 +471,7 @@
         out_shape=(big, big, big, small, small),
         in_specs=[hbm] * 3 + [vmem] * 2,
         out_specs=(hbm, hbm, hbm, vmem, vmem),
-        scratch_shapes=[pltpu.VMEM((3,) + q_raw.shape[1:], bf), dma((2, 3, 2))],
+        scratch_shapes=[pltpu.VMEM((3,) + q_raw.shape[1:], bf), dma((2, 3, 4))],
         name="hand_over",
     )(oq, ok, ov, gq, gk)
     return oq, ok, ov, gq.reshape(HD), gk.reshape(HD)

time: 114 us -> 112 us (0.982)
  Pallas kernels: 113 us -> 110 us
    pallas_call x1, Pallas kernels: 109 us -> 106 us  [on_device(): pl.pallas_call(functools.partial(kernel, nx, ny, ndp), out_shape=(big, bi...]
where the time goes in v4:
time: 112 us; the launch traced here: 111 us
  Pallas kernels  110 us (98%)
    pallas_call x1, Pallas kernels, on_device(): pl.pallas_call(functools.partial(kernel, nx, ny, ndp), out_shape=(big, bi...  106 us
    pallas_call x1, Pallas kernels, on_device(): pl.pallas_call(hand_over, out_shape=(big, big, big, small, small), in_spe...  4.01 us

profile of v4, /device:TPU:1, one launch (start us, length us, event | category | flops | bytes accessed | tf_op | source)
XLA Modules:
  0.0 110.9 jit_solution(482123832598476211)
XLA Ops:
  0.6 106.3 %attention_backward.1 = (bf16[1,256,2048]{2,1,0:T(8,128)(2,1)}, bf16[1,256,2048]{2,1,0:T(8,128)(2,1)}, bf16[1,256,2048]{2,1,0:T(8,128)(2,1)}, f32[1,128]{1,0:T(1,128)}, f32[1,128]{1,0:T(1,128)}) custom-call(bf16[1,256,2048]{2,1,0:T(8,128)(2,1)} %q_in.1, bf16[1,256,2048]{2,1,0:T(8,128)(2,1)} %k_in.1, bf16[1,256,2048]{2,1,0:T(8,128)(2,1)} %d_in.1, ...), custom_call_target="tpu_custom_call" | custom-call | flops 10737418240 | bytes 7340032 | tf_op jit(solution)/shard_map/attention_backward/pallas_call | solution.py:427
  106.9 4.0 %hand_over.1 = (bf16[1,256,2048]{2,1,0:T(8,128)(2,1)}, bf16[1,256,2048]{2,1,0:T(8,128)(2,1)}, bf16[1,256,2048]{2,1,0:T(8,128)(2,1)}, f32[1,128]{1,0:T(1,128)}, f32[1,128]{1,0:T(1,128)}) custom-call(bf16[1,256,2048]{2,1,0:T(8,128)(2,1)} %get-tuple-element.15.q, bf16[1,256,2048]{2,1,0:T(8,128)(2,1)} %get-tuple-element.16.k, ...), custom_call_target="tpu_custom_call" | custom-call | tf_op jit(solution)/shard_map/hand_over/pallas_call | solution.py:469
